TPU v7x, 512 devices: a whole 4x8x8 slice. The times are simulated.
512 devices in a mesh: section: 32 (over z_lo, y), dp: 16 (over z_hi, x, core).
Axes of the slice: x: 4, y: 8, z: 8 (z_hi: 2, z_lo: 4; z = z_hi * 4 + z_lo), core: 2. Of those that a mesh axis runs over, the one named last changes fastest.
Arguments:
- section_inputs: bfloat16 [32, 4096, 4096], P('section', 'dp'), may hold values from -6 to 6
- grad_first: bfloat16 [32, 1024, 4096], P('section', 'dp'), may hold values from -6 to 6
- value_master: float32 [32, 4096, 512], P('section', 'dp'), may hold values from -4 to 4
- first_moment: bfloat16 [32, 4096, 512], P('section', 'dp'), may hold values from -3 to 3
- second_moment: bfloat16 [32, 4096, 512], P('section', 'dp'), may hold values from 0.099609375 to 10
- output_weight: bfloat16 [32, 512, 4096], P('section', None, 'dp'), may hold values from -0.25 to 0.25
Outputs:
- master_next: float32 [32, 4096, 512], P('section', 'dp')
- first_next: bfloat16 [32, 4096, 512], P('section', 'dp')
- second_next: bfloat16 [32, 4096, 512], P('section', 'dp')
All inputs are finite; a program needn't handle non-finite values.
Results may differ from a plain program's by a relative error of at most 0.012.
Values may be sent and summed in bfloat16 or wider, within the bound.
A program may use at most 64 MiB of HBM per device.

v0:
```python
import math

import jax
import jax.numpy as jnp
from jax import lax
from jax.sharding import PartitionSpec as P

D = 4096
MB = 64
MICRO = 4


def from_behind(x, axis, by):
    devices = lax.axis_size(axis)
    return lax.ppermute(x, axis, [(i, (i + by) % devices) for i in range(devices)])


def on_device(section_inputs, grad_first, value_master, first_moment, second_moment, output_weight):
    scale = 1.0 / math.sqrt(D)
    master = value_master[0]
    weight = lax.all_gather(master.astype(jnp.bfloat16), "dp", axis=0, tiled=True)
    out_w = lax.all_gather(output_weight[0], "dp", axis=1, tiled=True)
    tokens = section_inputs[0]
    rinv_all = lax.rsqrt(
        jnp.mean(jnp.square(tokens.astype(jnp.float32)), axis=-1, keepdims=True) + 1e-05
    )
    grads = grad_first[0]
    hidden_list = []
    delta_list = []
    for step in range(MICRO):
        x_step = tokens[step * MB : (step + 1) * MB].astype(jnp.float32)
        rinv = rinv_all[step * MB : (step + 1) * MB]
        normed = x_step * rinv
        hidden = normed.astype(jnp.bfloat16)
        upper = jnp.dot(hidden, weight, preferred_element_type=jnp.float32) * scale
        back = lax.dot_general(
            grads, out_w, (((1,), (1,)), ((), ())), preferred_element_type=jnp.float32
        )
        sig = jax.nn.sigmoid(upper)
        delta = (back * sig * (1.0 + upper * (1.0 - sig))).astype(jnp.bfloat16)
        hidden_list.append(hidden)
        delta_list.append(delta)
        if step + 1 < MICRO:
            dh = (
                lax.dot_general(
                    delta, weight, (((1,), (1,)), ((), ())), preferred_element_type=jnp.float32
                )
                * scale
            )
            dx = grads.astype(jnp.float32) + rinv * (
                dh - normed * jnp.mean(normed * dh, axis=-1, keepdims=True)
            )
            grads = from_behind(dx.astype(jnp.bfloat16), "section", -1)
    hidden_all = jnp.concatenate(hidden_list, axis=0)
    delta_all = jnp.concatenate(delta_list, axis=0)
    whole = (
        lax.dot_general(
            hidden_all, delta_all, (((0,), (0,)), ((), ())), preferred_element_type=jnp.float32
        )
        * scale
    )
    grad = lax.psum_scatter(
        whole.astype(jnp.bfloat16), "dp", scatter_dimension=0, tiled=True
    ).astype(jnp.float32)
    moment_a = 0.9 * first_moment[0].astype(jnp.float32) + 0.1 * grad
    moment_b = 0.95 * second_moment[0].astype(jnp.float32) + 0.05 * grad * grad
    new_master = master - 0.02 * (moment_a / (jnp.sqrt(moment_b) + 1e-08) + 0.1 * master)
    return (
        new_master[None],
        moment_a.astype(jnp.bfloat16)[None],
        moment_b.astype(jnp.bfloat16)[None],
    )


def solution(mesh):
    in_specs = (
        P("section", "dp", None),
        P("section", "dp", None),
        P("section", "dp", None),
        P("section", "dp", None),
        P("section", "dp", None),
        P("section", None, "dp"),
    )
    out_specs = (P("section", "dp", None), P("section", "dp", None), P("section", "dp", None))
    return jax.shard_map(
        on_device, mesh=mesh, in_specs=in_specs, out_specs=out_specs, check_vma=False
    )
```

profile of v0, /device:TPU:1, one launch (start us, length us, event | category | flops | bytes accessed | tf_op | source)
XLA Modules:
  0.0 371.9 jit_solution(1855054328776824861)
XLA Ops:
  7.2 1.8 bitcast_convert_fusion
  9.8 2.1 multiply_reduce_fusion
  12.0 1.2 fusion.70
  13.2 87.8 %all-gather.4.cloned.1.call-done = bf16[4096,512]{1,0:T(8,128)(2,1)} async-done(((bf16[256,512]{1,0:T(8,128)(2,1)}), bf16[4096,512]{1,0:T(8,128)(2,1)}) %all-gather.4.cloned.1.call-update) | async-done | bytes 4194320 | tf_op jit(solution)/shard_map/all_gather | solution.py:21
  101.0 3.0 convolution_multiply_fusion.6
  104.1 79.9 %all-gather.6.cloned.1.call-done = bf16[1,512,4096]{2,1,0:T(8,128)(2,1)} async-done(((bf16[1,512,256]{2,1,0:T(8,128)(2,1)}), bf16[1,512,4096]{2,1,0:T(8,128)(2,1)}) %all-gather.6.cloned.1.call-update) | async-done | bytes 4194320 | tf_op jit(solution)/shard_map/all_gather | solution.py:22
  184.0 3.7 %fusion.48 = bf16[64,512]{1,0:T(8,128)(2,1)S(1)} fusion(bf16[1,512,4096]{2,1,0:T(8,128)(2,1)} %all-gather.6.cloned.1.call-done, bf16[1,64,4096]{2,1,0:T(8,128)(2,1)S(1)} %copy-done.3, f32[64,512]{1,0:T(8,128)S(1)} %convolution_multiply_fusion.6), kind=kOutput, calls=%fused_computation.35 | convolution fusion | flops 268730368 | bytes 4915200 | tf_op jit(solution)/shard_map/dot_general | solution.py:36
  187.8 1.5 fusion.71
  189.7 5.6 %collective-permute-start = (bf16[64,4096]{1,0:T(8,128)(2,1)S(1)}, bf16[64,4096]{1,0:T(8,128)(2,1)S(1)}, u32[]{:S(2)}, u32[]{:S(2)}) collective-permute-start(bf16[64,4096]{1,0:T(8,128)(2,1)S(1)} %get-tuple-element.7), channel_id=1, source_target_pairs={{0,496},{16,0},{32,16},{48,32},{64,48},{80,64},{96,80},{112,96},{1... | collective-permute-start | bytes 1572872 | tf_op jit(solution)/shard_map/ppermute | solution.py:15
  196.1 10.2 %collective-permute-done = bf16[64,4096]{1,0:T(8,128)(2,1)S(1)} collective-permute-done((bf16[64,4096]{1,0:T(8,128)(2,1)S(1)}, bf16[64,4096]{1,0:T(8,128)(2,1)S(1)}, u32[]{:S(2)}, u32[]{:S(2)}) %collective-permute-start) | collective-permute-done | bytes 524320 | tf_op jit(solution)/shard_map/ppermute | solution.py:15
  206.3 1.4 fusion.45
  207.7 1.5 fusion.63
  209.7 8.0 %collective-permute-start.1 = (bf16[64,4096]{1,0:T(8,128)(2,1)S(1)}, bf16[64,4096]{1,0:T(8,128)(2,1)S(1)}, u32[]{:S(2)}, u32[]{:S(2)}) collective-permute-start(bf16[64,4096]{1,0:T(8,128)(2,1)S(1)} %get-tuple-element.5), channel_id=1, source_target_pairs={{0,496},{16,0},{32,16},{48,32},{64,48},{80,64},{96,80},{112,96},{1... | collective-permute-start | bytes 1572872 | tf_op jit(solution)/shard_map/ppermute | solution.py:15
  217.7 0.8 convolution_multiply_fusion.4
  218.5 9.3 %collective-permute-done.1 = bf16[64,4096]{1,0:T(8,128)(2,1)S(1)} collective-permute-done((bf16[64,4096]{1,0:T(8,128)(2,1)S(1)}, bf16[64,4096]{1,0:T(8,128)(2,1)S(1)}, u32[]{:S(2)}, u32[]{:S(2)}) %collective-permute-start.1) | collective-permute-done | bytes 524320 | tf_op jit(solution)/shard_map/ppermute | solution.py:15
  227.8 1.4 fusion.42
  229.2 1.5 fusion.55
  231.2 8.0 %collective-permute-start.2 = (bf16[64,4096]{1,0:T(8,128)(2,1)S(1)}, bf16[64,4096]{1,0:T(8,128)(2,1)S(1)}, u32[]{:S(2)}, u32[]{:S(2)}) collective-permute-start(bf16[64,4096]{1,0:T(8,128)(2,1)S(1)} %get-tuple-element.3), channel_id=1, source_target_pairs={{0,496},{16,0},{32,16},{48,32},{64,48},{80,64},{96,80},{112,96},{1... | collective-permute-start | bytes 1572872 | tf_op jit(solution)/shard_map/ppermute | solution.py:15
  239.2 0.8 convolution_multiply_fusion.3
  240.0 8.4 %collective-permute-done.2 = bf16[64,4096]{1,0:T(8,128)(2,1)S(1)} collective-permute-done((bf16[64,4096]{1,0:T(8,128)(2,1)S(1)}, bf16[64,4096]{1,0:T(8,128)(2,1)S(1)}, u32[]{:S(2)}, u32[]{:S(2)}) %collective-permute-start.2) | collective-permute-done | bytes 524320 | tf_op jit(solution)/shard_map/ppermute | solution.py:15
  248.4 1.4 fusion.39
  249.8 2.8 multiply_convert_fusion
  252.7 110.3 %reduce-scatter.2.cloned.1.call-done = bf16[256,512]{1,0:T(8,128)(2,1)} async-done(((bf16[4096,512]{1,0:T(8,128)(2,1)}), bf16[256,512]{1,0:T(8,128)(2,1)}) %reduce-scatter.2.cloned.1.call-update) | async-done | bytes 262160 | tf_op jit(solution)/shard_map/reduce_scatter | solution.py:62
  363.0 2.4 fusion.84
  (29 shorter events, 3.1 us)
Async XLA Ops:
  7.2 93.9 %all-gather.4.cloned.1.call-start = ((), (), s32[]{:S(2)}) async-start(), calls=%async_computation.1 | async-start | bytes 4456448 | tf_op jit(solution)/shard_map/all_gather | solution.py:21
  9.0 175.0 %copy-start.3 = (bf16[1,64,4096]{2,1,0:T(8,128)(2,1)S(1)}, bf16[1,64,4096]{2,1,0:T(8,128)(2,1)}, u32[]{:S(2)}) copy-start(bf16[1,64,4096]{2,1,0:T(8,128)(2,1)} %param.7) | copy-start | bytes 1572868
  9.0 175.0 %all-gather.6.cloned.1.call-start = ((), (), s32[]{:S(2)}) async-start(), calls=%async_computation.3 | async-start | bytes 4456448 | tf_op jit(solution)/shard_map/all_gather | solution.py:22
  9.8 353.2 %reduce-scatter.2.cloned.1.call-start = ((), (), s32[]{:S(2)}) async-start(), calls=%async_computation.2 | async-start | bytes 4456448 | tf_op jit(solution)/shard_map/reduce_scatter | solution.py:62
  13.2 174.5 %copy-start.2 = (bf16[1,256,4096]{2,1,0:T(8,128)(2,1)S(1)}, bf16[1,256,4096]{2,1,0:T(8,128)(2,1)}, u32[]{:S(2)}) copy-start(bf16[1,256,4096]{2,1,0:T(8,128)(2,1)} %param.6) | copy-start | bytes 6291460
  184.0 3.7 %copy-start = (bf16[4096,512]{1,0:T(8,128)(2,1)S(1)}, bf16[4096,512]{1,0:T(8,128)(2,1)}, u32[]{:S(2)}) copy-start(bf16[4096,512]{1,0:T(8,128)(2,1)} %all-gather.4.cloned.1.call-done) | copy-start | bytes 12582916
  189.2 17.1 %copy-start.1 = (bf16[1,512,4096]{2,1,0:T(8,128)(2,1)S(1)}, bf16[1,512,4096]{2,1,0:T(8,128)(2,1)}, u32[]{:S(2)}) copy-start(bf16[1,512,4096]{2,1,0:T(8,128)(2,1)} %all-gather.6.cloned.1.call-done) | copy-start | bytes 12582916
  189.7 16.6 %collective-permute-start = (bf16[64,4096]{1,0:T(8,128)(2,1)S(1)}, bf16[64,4096]{1,0:T(8,128)(2,1)S(1)}, u32[]{:S(2)}, u32[]{:S(2)}) collective-permute-start(bf16[64,4096]{1,0:T(8,128)(2,1)S(1)} %get-tuple-element.7), channel_id=1, source_target_pairs={{0,496},{16,0},{32,16},{48,32},{64,48},{80,64},{96,80},{112,96},{1... | collective-permute-start | bytes 1572872 | tf_op jit(solution)/shard_map/ppermute | solution.py:15
  209.7 18.2 %collective-permute-start.1 = (bf16[64,4096]{1,0:T(8,128)(2,1)S(1)}, bf16[64,4096]{1,0:T(8,128)(2,1)S(1)}, u32[]{:S(2)}, u32[]{:S(2)}) collective-permute-start(bf16[64,4096]{1,0:T(8,128)(2,1)S(1)} %get-tuple-element.5), channel_id=1, source_target_pairs={{0,496},{16,0},{32,16},{48,32},{64,48},{80,64},{96,80},{112,96},{1... | collective-permute-start | bytes 1572872 | tf_op jit(solution)/shard_map/ppermute | solution.py:15
  231.2 17.2 %collective-permute-start.2 = (bf16[64,4096]{1,0:T(8,128)(2,1)S(1)}, bf16[64,4096]{1,0:T(8,128)(2,1)S(1)}, u32[]{:S(2)}, u32[]{:S(2)}) collective-permute-start(bf16[64,4096]{1,0:T(8,128)(2,1)S(1)} %get-tuple-element.3), channel_id=1, source_target_pairs={{0,496},{16,0},{32,16},{48,32},{64,48},{80,64},{96,80},{112,96},{1... | collective-permute-start | bytes 1572872 | tf_op jit(solution)/shard_map/ppermute | solution.py:15
  252.6 110.3 %copy-start.4 = (f32[1,256,512]{2,1,0:T(8,128)S(1)}, f32[1,256,512]{2,1,0:T(8,128)}, u32[]{:S(2)}) copy-start(f32[1,256,512]{2,1,0:T(8,128)} %param.8) | copy-start | bytes 1572868
  252.6 110.3 %copy-start.5 = (bf16[1,256,512]{2,1,0:T(8,128)(2,1)S(1)}, bf16[1,256,512]{2,1,0:T(8,128)(2,1)}, u32[]{:S(2)}) copy-start(bf16[1,256,512]{2,1,0:T(8,128)(2,1)} %param.10) | copy-start | bytes 786436
  252.6 110.3 %copy-start.6 = (bf16[1,256,512]{2,1,0:T(8,128)(2,1)S(1)}, bf16[1,256,512]{2,1,0:T(8,128)(2,1)}, u32[]{:S(2)}) copy-start(bf16[1,256,512]{2,1,0:T(8,128)(2,1)} %param.9) | copy-start | bytes 786436
Sparse Core Ops, SparseCore 0:
  11.9 89.0 all-gather.3
  104.2 79.7 all-gather.5
  252.8 110.1 reduce-scatter.1
where the time goes:
time: 373 us; the launch traced here: 372 us
  waiting for transfers between devices  307 us (82%)
  starting transfers between devices  21.7 us (6%)
  matrix products  20.7 us (6%)
  between operations  13.9 us (4%)
  other arithmetic  8.76 us (2%)
    reduce_scatter x1, waiting for transfers between devices, on_device(): lax.psum_scatter(whole.astype(jnp.bfloat16), 'dp', scatter_dimension=0, t...  110 us
    all_gather x1, waiting for transfers between devices, on_device(): lax.all_gather(master.astype(jnp.bfloat16), 'dp', axis=0, tiled=True)  87.8 us
    all_gather x1, waiting for transfers between devices, on_device(): out_w = lax.all_gather(output_weight[0], 'dp', axis=1, tiled=True)  79.9 us
    ppermute x3, waiting for transfers between devices, from_behind(): lax.ppermute(x, axis, [(i, (i + by) % devices) for i in range(devices)])  27.9 us
    ppermute x3, starting transfers between devices, from_behind(): lax.ppermute(x, axis, [(i, (i + by) % devices) for i in range(devices)])  21.6 us
    dot_general x4, matrix products, on_device(): lax.dot_general(grads, out_w, (((1,), (1,)), ((), ())), preferred_element...  7.92 us
  transfers between devices with their start and end apart: 6, of which 6 were waited for; matrix products, arithmetic and copies ran while one was open for 2% of the time, Pallas kernels for 0%

commit v1 on v0

v1 whole, which is shorter than its diff:
```python
import math

import jax
import jax.numpy as jnp
from jax import lax
from jax.experimental import pallas as pl
from jax.experimental.pallas import tpu as pltpu
from jax.sharding import PartitionSpec as P

MESH = pl.DeviceIdType.MESH
BF16 = jnp.bfloat16
F32 = jnp.float32

D = 4096
R = 512
TOK = 256
ROW = 32
STAGES = TOK // ROW
N_DP = 16
SECTIONS = 32
BLK = D // N_DP
CHUNKS = 4
WIDE = D // CHUNKS
PER = WIDE // BLK
HALF = 8
SCALE = 1.0 / math.sqrt(D)

NT = (((1,), (1,)), ((), ()))
TN = (((0,), (0,)), ((), ()))


def lap_kernel(
    x_hbm, g_hbm, m_hbm, first_hbm, second_hbm, ow_hbm,
    master_out, first_out, second_out,
    x_v, g_v, m_v, first_v, second_v, w_all, o_all, h_v, rinv_v, u_v, f_v, back_v,
    du_all, h_got, acc, z_out, z_in, dx_v,
    local_sem, ag_send, ag_recv, relay_send, relay_recv, h_send, h_recv,
    du_send, du_recv, z_send, z_recv,
):
    s = lax.axis_index("section")
    d = lax.axis_index("dp")
    zh, x, c = d // 8, (d // 2) % 4, d % 2
    me8 = d % 8

    def dp_of(zsel, dx, flip):
        z = zh if zsel == 0 else 1 - zh
        core = c if flip == 0 else 1 - c
        return z * 8 + ((x + dx + 4) % 4) * 2 + core

    def on_dp(zsel, dx, flip):
        return (s, dp_of(zsel, dx, flip))

    behind = ((s + SECTIONS - 1) % SECTIONS, d)
    ahead = ((s + 1) % SECTIONS, d)
    right, left = on_dp(0, 1, 0), on_dp(0, -1, 0)
    sibling, across = on_dp(0, 0, 1), on_dp(1, 0, 0)

    loads = {}

    def load(name, src, dst, at):
        loads[name] = pltpu.make_async_copy(src, dst, local_sem.at[at])
        loads[name].start()

    load("m", m_hbm.at[0], m_v, 0)
    load("ow", ow_hbm.at[0], o_all.at[d], 1)
    load("x", x_hbm.at[0], x_v, 2)
    for t in range(2):
        for n in range(CHUNKS):
            load(
                ("g", t, n),
                g_hbm.at[0, pl.ds(t * ROW, ROW), pl.ds(n * WIDE, WIDE)],
                g_v.at[t, n],
                5 + t * CHUNKS + n,
            )
    load("first", first_hbm.at[0], first_v, 3)
    load("second", second_hbm.at[0], second_v, 4)

    barrier = pltpu.get_barrier_semaphore()
    greet = [behind, ahead, across] + [(s, zh * 8 + (me8 + i) % 8) for i in range(1, 8)]
    for other in greet:
        pl.semaphore_signal(barrier, inc=1, device_id=other, device_id_type=MESH)

    loads["m"].wait()
    w_all[d] = m_v[...].astype(BF16)
    loads["ow"].wait()
    pl.semaphore_wait(barrier, len(greet))

    sends = []

    def piece(p, owner):
        if p < 2:
            return w_all.at[owner, pl.ds(p * (BLK // 2), BLK // 2)]
        return o_all.at[owner, pl.ds((p - 2) * (R // 2), R // 2)]

    def pass_on(p, owner, target):
        copy = pltpu.make_async_remote_copy(
            src_ref=piece(p, owner), dst_ref=piece(p, owner),
            send_sem=ag_send.at[len(sends)], recv_sem=ag_recv.at[p, owner],
            device_id=target, device_id_type=MESH,
        )
        copy.start()
        sends.append(copy)

    def arrived(p, owner):
        pltpu.make_async_remote_copy(
            src_ref=piece(p, owner), dst_ref=piece(p, owner),
            send_sem=ag_send.at[0], recv_sem=ag_recv.at[p, owner],
            device_id=sibling, device_id_type=MESH,
        ).wait_recv()

    for p in range(4):
        for target in (across, right, left, sibling):
            pass_on(p, d, target)

    def handle(p, zsel, dx):
        owner = dp_of(zsel, dx, 0)
        arrived(p, owner)
        if dx == 0 or (dx == -1 and p % 2 == 0):
            pass_on(p, owner, right)
        if dx == 0 or (dx == 1 and p % 2 == 1):
            pass_on(p, owner, left)
        pass_on(p, owner, sibling)

    def from_sibling(pieces, zsel):
        for p in pieces:
            for dx in (0, 1, -1, 2):
                arrived(p, dp_of(zsel, dx, 1))

    loads["x"].wait()

    def normalise(t, carry):
        xs = x_v[pl.ds(pl.multiple_of(t * ROW, ROW), ROW), :].astype(F32)
        rinv = lax.rsqrt(jnp.sum(xs * xs, axis=-1, keepdims=True) * (1.0 / D) + 1e-05)
        rinv_v[t] = rinv
        hidden = (xs * rinv).astype(BF16)
        for j in range(N_DP):
            h_v[j, t] = hidden[:, j * BLK : (j + 1) * BLK]
        return carry

    lax.fori_loop(0, STAGES, normalise, 0)
    u_v[...] = jnp.zeros_like(u_v)
    back_v[...] = jnp.zeros_like(back_v)
    for t in range(2):
        for n in range(CHUNKS):
            loads["g", t, n].wait()

    def upper(zsel):
        base = (zh if zsel == 0 else 1 - zh) * HALF

        def one(i, carry):
            j = base + i
            part = jnp.dot(
                h_v[j].reshape(TOK, BLK), w_all[j], preferred_element_type=F32
            )
            u_v[...] += part.reshape(STAGES, ROW, R)
            return carry

        lax.fori_loop(0, HALF, one, 0)

    def onto(total, grads, n):
        for i in range(PER):
            total = total + lax.dot_general(
                grads[:, i * BLK : (i + 1) * BLK], o_all[n * PER + i], NT,
                preferred_element_type=F32,
            )
        return total

    def first_back(zsel):
        base = (zh if zsel == 0 else 1 - zh) * (HALF // PER)

        def one(i, carry):
            n = base + i
            total = back_v[...].reshape(2 * ROW, R)
            grads = g_v[0:2, n].reshape(2 * ROW, WIDE)
            back_v[...] = onto(total, grads, n).reshape(2, ROW, R)
            return carry

        lax.fori_loop(0, HALF // PER, one, 0)

    for event in (
        (0, 0, -1), (0, 0, 1), (1, 0, -1), (1, 0, 1), (0, 1, 0),
        (2, 0, -1), (2, 0, 1), (3, 0, -1), (3, 0, 1), (0, 0, 2), (1, 1, 0), (1, 0, 2),
    ):
        handle(*event)
    from_sibling((0, 1), 0)
    upper(0)
    for event in (
        (2, 0, 2), (3, 0, 2), (0, 1, -1), (0, 1, 1), (2, 1, 0),
        (1, 1, -1), (1, 1, 1), (0, 1, 2), (1, 1, 2),
    ):
        handle(*event)
    from_sibling((2, 3), 0)
    first_back(0)
    for event in ((3, 1, 0), (2, 1, -1), (2, 1, 1)):
        handle(*event)
    from_sibling((0, 1), 1)
    upper(1)

    def gate(t, carry):
        u = u_v[t] * SCALE
        sig = jax.nn.sigmoid(u)
        u_v[t] = u
        f_v[t] = sig * (1.0 + u * (1.0 - sig))
        return carry

    lax.fori_loop(0, STAGES, gate, 0)
    for event in ((2, 1, 2), (3, 1, -1), (3, 1, 1), (3, 1, 2)):
        handle(*event)
    from_sibling((2, 3), 1)
    first_back(1)

    def relay_copy(t, n):
        return pltpu.make_async_remote_copy(
            src_ref=dx_v.at[t, n], dst_ref=g_v.at[t + 2, n],
            send_sem=relay_send.at[t, n], recv_sem=relay_recv.at[t, n],
            device_id=behind, device_id_type=MESH,
        )

    def du_copy(t, i):
        return pltpu.make_async_remote_copy(
            src_ref=du_all.at[t, me8], dst_ref=du_all.at[t, me8],
            send_sem=du_send.at[t, i], recv_sem=du_recv.at[t, i],
            device_id=(s, zh * 8 + (me8 + i) % 8), device_id_type=MESH,
        )

    def du_arrived(t, i):
        src = (me8 + 8 - i) % 8
        pltpu.make_async_remote_copy(
            src_ref=du_all.at[t, src], dst_ref=du_all.at[t, src],
            send_sem=du_send.at[t, i], recv_sem=du_recv.at[t, i],
            device_id=sibling, device_id_type=MESH,
        ).wait_recv()

    def stage(t, arrives, leaves):
        if arrives:

            def take(n, total):
                relay_copy(t - 2, n).wait_recv()
                return onto(total, g_v[t, n], n)

            back = lax.fori_loop(0, CHUNKS, take, jnp.zeros((ROW, R), F32))
        else:
            back = back_v[t]
        du = (back * f_v[t]).astype(BF16)
        du_all[t, me8] = du
        if leaves:
            rinv = rinv_v[t]
            coef = jnp.sum(du.astype(F32) * u_v[t], axis=-1, keepdims=True) * (1.0 / D)
            coef = coef * rinv * rinv
            gain = rinv * SCALE
            rows = pl.ds(pl.multiple_of(t * ROW, ROW), ROW)

            def give(n, carry):
                wide = w_all[pl.ds(n * PER, PER)].reshape(WIDE, R)
                dh = lax.dot_general(du, wide, NT, preferred_element_type=F32)
                xs = x_v[rows, pl.ds(pl.multiple_of(n * WIDE, WIDE), WIDE)].astype(F32)
                dx = g_v[t, n].astype(F32) + gain * dh - xs * coef
                dx_v[t, n] = dx.astype(BF16)
                relay_copy(t, n).start()
                return carry

            lax.fori_loop(0, CHUNKS, give, 0)
        for i in range(1, 8):
            du_copy(t, i).start()

    def plain(arrives, leaves):
        def one(t, carry):
            stage(t, arrives, leaves)
            return carry

        return one

    lax.fori_loop(0, 2, plain(False, True), 0)

    def h_copy(i, zsel):
        to = (me8 + i) % 8
        block = (zh if zsel == 0 else 1 - zh) * 8 + to
        return pltpu.make_async_remote_copy(
            src_ref=h_v.at[block], dst_ref=h_got.at[zsel, :, me8],
            send_sem=h_send.at[i, zsel], recv_sem=h_recv.at[i, zsel],
            device_id=(s, zh * 8 + to), device_id_type=MESH,
        )

    def h_arrived(i, zsel):
        src = (me8 + 8 - i) % 8
        pltpu.make_async_remote_copy(
            src_ref=h_v.at[0], dst_ref=h_got.at[zsel, :, src],
            send_sem=h_send.at[i, zsel], recv_sem=h_recv.at[i, zsel],
            device_id=sibling, device_id_type=MESH,
        ).wait_recv()

    for i in range(1, 8):
        for zsel in range(2):
            h_copy(i, zsel).start()
    for zsel in range(2):
        h_got[zsel, :, me8] = h_v[dp_of(zsel, 0, 0)]

    lax.fori_loop(2, 6, plain(True, True), 0)
    acc[...] = jnp.zeros_like(acc)

    def gradient(t, carry):
        for i in range(1, 8):
            du_arrived(t, i)
        du = du_all[t].reshape(HALF * ROW, R)
        for zsel in (1, 0):
            acc[zsel] += lax.dot_general(
                h_got[zsel, t].reshape(HALF * ROW, BLK), du, TN,
                preferred_element_type=F32,
            )
        return carry

    for i in range(1, 8):
        for zsel in range(2):
            h_arrived(i, zsel)
    lax.fori_loop(0, 4, gradient, 0)
    stage(6, True, False)
    lax.fori_loop(4, 6, gradient, 0)
    stage(7, True, False)
    lax.fori_loop(6, 8, gradient, 0)

    def z_copy(i):
        part = pl.ds(i * (BLK // 2), BLK // 2)
        return pltpu.make_async_remote_copy(
            src_ref=z_out.at[part], dst_ref=z_in.at[part],
            send_sem=z_send.at[i], recv_sem=z_recv.at[i],
            device_id=across, device_id_type=MESH,
        )

    for i in range(2):
        part = pl.ds(i * (BLK // 2), BLK // 2)
        z_out[part] = (acc[1, part] * SCALE).astype(BF16)
        z_copy(i).start()
    loads["first"].wait()
    loads["second"].wait()
    for i in range(2):
        part = pl.ds(i * (BLK // 2), BLK // 2)
        z_copy(i).wait_recv()
        grad = acc[0, part] * SCALE + z_in[part].astype(F32)
        moment_a = 0.9 * first_v[part].astype(F32) + 0.1 * grad
        moment_b = 0.95 * second_v[part].astype(F32) + 0.05 * grad * grad
        master = m_v[part]
        master_out[part] = master - 0.02 * (
            moment_a / (jnp.sqrt(moment_b) + 1e-08) + 0.1 * master
        )
        first_out[part] = moment_a.astype(BF16)
        second_out[part] = moment_b.astype(BF16)

    for copy in sends:
        copy.wait_send()

    def sent(t, carry):
        for i in range(1, 8):
            du_copy(t, i).wait_send()
        return carry

    def relayed(t, carry):
        for n in range(CHUNKS):
            relay_copy(t, n).wait_send()
        return carry

    lax.fori_loop(0, STAGES, sent, 0)
    lax.fori_loop(0, 6, relayed, 0)
    for i in range(1, 8):
        for zsel in range(2):
            h_copy(i, zsel).wait_send()
    for i in range(2):
        z_copy(i).wait_send()


def on_device(section_inputs, grad_first, value_master, first_moment, second_moment, output_weight):
    dma = pltpu.SemaphoreType.DMA
    outs = pl.pallas_call(
        lap_kernel,
        name="lap",
        out_shape=(
            jax.ShapeDtypeStruct((BLK, R), F32),
            jax.ShapeDtypeStruct((BLK, R), BF16),
            jax.ShapeDtypeStruct((BLK, R), BF16),
        ),
        in_specs=[pl.BlockSpec(memory_space=pl.ANY)] * 6,
        out_specs=[pl.BlockSpec(memory_space=pltpu.VMEM)] * 3,
        scratch_shapes=[
            pltpu.VMEM((TOK, D), BF16),
            pltpu.VMEM((STAGES, CHUNKS, ROW, WIDE), BF16),
            pltpu.VMEM((BLK, R), F32),
            pltpu.VMEM((BLK, R), BF16),
            pltpu.VMEM((BLK, R), BF16),
            pltpu.VMEM((N_DP, BLK, R), BF16),
            pltpu.VMEM((N_DP, R, BLK), BF16),
            pltpu.VMEM((N_DP, STAGES, ROW, BLK), BF16),
            pltpu.VMEM((STAGES, ROW, 1), F32),
            pltpu.VMEM((STAGES, ROW, R), F32),
            pltpu.VMEM((STAGES, ROW, R), F32),
            pltpu.VMEM((2, ROW, R), F32),
            pltpu.VMEM((STAGES, HALF, ROW, R), BF16),
            pltpu.VMEM((2, STAGES, HALF, ROW, BLK), BF16),
            pltpu.VMEM((2, BLK, R), F32),
            pltpu.VMEM((BLK, R), BF16),
            pltpu.VMEM((BLK, R), BF16),
            pltpu.VMEM((6, CHUNKS, ROW, WIDE), BF16),
            dma((5 + 2 * CHUNKS,)),
            dma((64,)),
            dma((4, N_DP)),
            dma((6, CHUNKS)),
            dma((6, CHUNKS)),
            dma((8, 2)),
            dma((8, 2)),
            dma((STAGES, 8)),
            dma((STAGES, 8)),
            dma((2,)),
            dma((2,)),
        ],
        compiler_params=pltpu.CompilerParams(
            collective_id=0, has_side_effects=True, vmem_limit_bytes=48 * 1024 * 1024
        ),
        cost_estimate=pl.CostEstimate(flops=4 * 10**9, bytes_accessed=5 * 2**20, transcendentals=0),
    )(section_inputs, grad_first, value_master, first_moment, second_moment, output_weight)
    return tuple(out[None] for out in outs)


def solution(mesh):
    rows = P("section", "dp", None)
    return jax.shard_map(
        on_device,
        mesh=mesh,
        in_specs=(rows, rows, rows, rows, rows, P("section", None, "dp")),
        out_specs=(rows, rows, rows),
        check_vma=False,
    )
```

time: 373 us -> 139 us (0.37)
  waiting for transfers between devices: 307 us -> 0 us
  Pallas kernels: 0 us -> 129 us
  starting transfers between devices: 21.7 us -> 0 us
  matrix products: 20.7 us -> 0 us
  between operations: 13.9 us -> 0.65 us
  other arithmetic: 8.76 us -> 0 us
  local copies, waits for them, and re-layouts: 0.11 us -> 8.71 us
    all_gather x2 -> x0, waiting for transfers between devices: 168 us -> none  [the longest x1 87.8 us: on_device(): lax.all_gather(master.astype(jnp.bfloat16), 'dp', axis=0, tiled=True)]
    pallas_call x0 -> x1, Pallas kernels: none -> 129 us  [on_device(): pl.pallas_call(lap_kernel, name='lap', out_shape=(jax.ShapeDtypeStruct((B...]
    reduce_scatter x1 -> x0, waiting for transfers between devices: 110 us -> none  [on_device(): lax.psum_scatter(whole.astype(jnp.bfloat16), 'dp', scatter_dimension=0, t...]
    ppermute x3 -> x0, waiting for transfers between devices: 27.9 us -> none  [from_behind(): lax.ppermute(x, axis, [(i, (i + by) % devices) for i in range(devices)])]
    ppermute x3 -> x0, starting transfers between devices: 21.6 us -> none  [from_behind(): lax.ppermute(x, axis, [(i, (i + by) % devices) for i in range(devices)])]
    dot_general x12 -> x0, matrix products: 20.7 us -> none  [the longest x4 7.92 us: on_device(): lax.dot_general(grads, out_w, (((1,), (1,)), ((), ())), preferred_element...]
    unnamed x14 -> x15, local copies, waits for them, and re-layouts: 0.03 us -> 8.71 us
    convert_element_type x5 -> x0, other arithmetic: 4.28 us -> none  [the longest x1 1.78 us: on_device(): master.astype(jnp.bfloat16)]
  transfers between devices with their start and end apart: 6 -> 0, of which waited for: 6 -> 0; matrix products, arithmetic and copies ran while one was open for 2% -> 0% of each run, Pallas kernels for 0% -> 0%
where the time goes in v1:
time: 139 us; the launch traced here: 138 us
  Pallas kernels  129 us (93%)
  local copies, waits for them, and re-layouts  8.71 us (6%)
    pallas_call x1, Pallas kernels, on_device(): pl.pallas_call(lap_kernel, name='lap', out_shape=(jax.ShapeDtypeStruct((B...  129 us
    unnamed x15, local copies, waits for them, and re-layouts  8.71 us

profile of v1, /device:TPU:1, one launch (start us, length us, event | category | flops | bytes accessed | tf_op | source)
XLA Modules:
  0.0 138.2 jit_solution(9122047020908933152)
XLA Ops:
  0.6 0.0 copy-start
  0.6 1.6 %copy-done = bf16[1,256,4096]{2,1,0:T(8,128)(2,1)S(1)} copy-done((bf16[1,256,4096]{2,1,0:T(8,128)(2,1)S(1)}, bf16[1,256,4096]{2,1,0:T(8,128)(2,1)}, u32[]{:S(2)}) %copy-start) | copy-done | bytes 2097176
  2.2 0.0 copy-start.1
  2.2 1.0 copy-done.1
  3.3 0.0 copy-start.2
  3.3 1.0 copy-done.2
  4.3 0.0 copy-start.3
  4.3 0.9 copy-done.3
  5.3 0.0 copy-start.4
  5.3 0.9 copy-done.4
  6.2 0.0 copy-start.5
  6.2 0.9 copy-done.5
  7.2 128.9 %lap.1 = (f32[256,512]{1,0:T(8,128)S(1)}, bf16[256,512]{1,0:T(8,128)(2,1)S(1)}, bf16[256,512]{1,0:T(8,128)(2,1)S(1)}) custom-call(bf16[1,256,4096]{2,1,0:T(8,128)(2,1)S(1)} %copy-done, bf16[1,64,4096]{2,1,0:T(8,128)(2,1)S(1)} %copy-done.1, f32[1,256,512]{2,1,0:T(8,128)S(1)} %copy-done.2, bf16[1,256,512]{2,1,0:T(8,128)(2,1)S(1)} %copy-done.3, ...), custom_call_target="tpu_custom_call" | custom-call | flops 4000000000 | bytes 5242880 | tf_op jit(solution)/shard_map/lap/pallas_call | solution.py:372
  136.0 0.8 copy.12
  136.8 0.7 copy.13
  137.5 0.7 copy.14
Async XLA Ops:
  0.6 1.6 %copy-start = (bf16[1,256,4096]{2,1,0:T(8,128)(2,1)S(1)}, bf16[1,256,4096]{2,1,0:T(8,128)(2,1)}, u32[]{:S(2)}) copy-start(bf16[1,256,4096]{2,1,0:T(8,128)(2,1)} %x_hbm.1) | copy-start | bytes 6291460
  2.2 1.0 copy-start.1
  3.3 1.0 copy-start.2
  4.3 0.9 copy-start.3
  5.3 0.9 copy-start.4
  6.2 0.9 copy-start.5

commit v2 on v1

--- a/solution.py
+++ b/solution.py
@@ -23,6 +23,8 @@
 WIDE = D // CHUNKS
 PER = WIDE // BLK
 HALF = 8
+EARLY = 6
+LATE = STAGES - EARLY
 SCALE = 1.0 / math.sqrt(D)
 
 NT = (((1,), (1,)), ((), ()))
@@ -30,12 +32,12 @@
 
 
 def lap_kernel(
-    x_hbm, g_hbm, m_hbm, first_hbm, second_hbm, ow_hbm,
-    master_out, first_out, second_out,
-    x_v, g_v, m_v, first_v, second_v, w_all, o_all, h_v, rinv_v, u_v, f_v, back_v,
-    du_all, h_got, acc, z_out, z_in, dx_v,
+    x_hbm, g_hbm, m_hbm, ow_hbm, grad_out,
+    x_v, g_v, m_v, w_all, o_all, h_v, rinv_v, u_v, f_v, back_v,
+    du_all, du_far, h_got, h_cross, h_far, acc, z_out, z_in, dx_v,
     local_sem, ag_send, ag_recv, relay_send, relay_recv, h_send, h_recv,
-    du_send, du_recv, z_send, z_recv,
+    du_send, du_recv, cross_send, cross_recv, far_send, far_recv, hf_send, hf_recv,
+    z_send, z_recv,
 ):
     s = lax.axis_index("section")
     d = lax.axis_index("dp")
@@ -70,10 +72,8 @@
                 ("g", t, n),
                 g_hbm.at[0, pl.ds(t * ROW, ROW), pl.ds(n * WIDE, WIDE)],
                 g_v.at[t, n],
-                5 + t * CHUNKS + n,
+                3 + t * CHUNKS + n,
             )
-    load("first", first_hbm.at[0], first_v, 3)
-    load("second", second_hbm.at[0], second_v, 4)
 
     barrier = pltpu.get_barrier_semaphore()
     greet = [behind, ahead, across] + [(s, zh * 8 + (me8 + i) % 8) for i in range(1, 8)]
@@ -176,6 +176,12 @@
             return carry
 
         lax.fori_loop(0, HALF // PER, one, 0)
+
+    hidden_across = pltpu.make_async_remote_copy(
+        src_ref=h_v.at[pl.ds((1 - zh) * HALF, HALF), pl.ds(EARLY, LATE)], dst_ref=h_cross,
+        send_sem=hf_send.at[0], recv_sem=hf_recv.at[0],
+        device_id=across, device_id_type=MESH,
+    )
 
     for event in (
         (0, 0, -1), (0, 0, 1), (1, 0, -1), (1, 0, 1), (0, 1, 0),
@@ -191,7 +197,9 @@
         handle(*event)
     from_sibling((2, 3), 0)
     first_back(0)
-    for event in ((3, 1, 0), (2, 1, -1), (2, 1, 1)):
+    handle(3, 1, 0)
+    hidden_across.start()
+    for event in ((2, 1, -1), (2, 1, 1)):
         handle(*event)
     from_sibling((0, 1), 1)
     upper(1)
@@ -216,20 +224,52 @@
             device_id=behind, device_id_type=MESH,
         )
 
-    def du_copy(t, i):
-        return pltpu.make_async_remote_copy(
-            src_ref=du_all.at[t, me8], dst_ref=du_all.at[t, me8],
-            send_sem=du_send.at[t, i], recv_sem=du_recv.at[t, i],
-            device_id=(s, zh * 8 + (me8 + i) % 8), device_id_type=MESH,
-        )
-
-    def du_arrived(t, i):
-        src = (me8 + 8 - i) % 8
-        pltpu.make_async_remote_copy(
+    def mate(i):
+        return (s, zh * 8 + (me8 + i) % 8)
+
+    sib8 = 2 * x + 1 - c
+
+    def du_copy(t, src, i, target):
+        return pltpu.make_async_remote_copy(
             src_ref=du_all.at[t, src], dst_ref=du_all.at[t, src],
-            send_sem=du_send.at[t, i], recv_sem=du_recv.at[t, i],
-            device_id=sibling, device_id_type=MESH,
-        ).wait_recv()
+            send_sem=du_send.at[t, i], recv_sem=du_recv.at[t, src],
+            device_id=target, device_id_type=MESH,
+        )
+
+    def rail(t):
+        return [du_copy(t, me8, i, mate(2 * i)) for i in (1, 3, 2)] + [
+            du_copy(t, me8, 0, sibling)
+        ]
+
+    def spread(t):
+        return [du_copy(t, me8, i, mate(i)) for i in range(1, 8)]
+
+    def passed(t):
+        return [du_copy(t, (me8 + 2 * i) % 8, 3 + i, sibling) for i in (1, 3, 2)]
+
+    def pass_rail(t):
+        for copy in passed(t):
+            copy.wait_recv()
+            copy.start()
+
+    def cross_copy(k):
+        return pltpu.make_async_remote_copy(
+            src_ref=du_all.at[EARLY + k, me8], dst_ref=du_far.at[k, me8],
+            send_sem=cross_send.at[k], recv_sem=cross_recv.at[k],
+            device_id=across, device_id_type=MESH,
+        )
+
+    def far_copy(k, i, src):
+        return pltpu.make_async_remote_copy(
+            src_ref=du_far.at[k, src], dst_ref=du_far.at[k, src],
+            send_sem=far_send.at[k, i], recv_sem=far_recv.at[k, src],
+            device_id=mate(i), device_id_type=MESH,
+        )
+
+    def spread_far(k):
+        cross_copy(k).wait_recv()
+        for i in range(1, 8):
+            far_copy(k, i, me8).start()
 
     def stage(t, arrives, leaves):
         if arrives:
@@ -260,47 +300,51 @@
                 return carry
 
             lax.fori_loop(0, CHUNKS, give, 0)
-        for i in range(1, 8):
-            du_copy(t, i).start()
+        return du
 
     def plain(arrives, leaves):
         def one(t, carry):
             stage(t, arrives, leaves)
+            for copy in rail(t):
+                copy.start()
             return carry
 
         return one
 
-    lax.fori_loop(0, 2, plain(False, True), 0)
-
-    def h_copy(i, zsel):
+    def h_copy(i, zsel, src):
         to = (me8 + i) % 8
         block = (zh if zsel == 0 else 1 - zh) * 8 + to
-        return pltpu.make_async_remote_copy(
-            src_ref=h_v.at[block], dst_ref=h_got.at[zsel, :, me8],
+        count = STAGES if zsel == 0 else EARLY
+        return pltpu.make_async_remote_copy(
+            src_ref=h_v.at[block, pl.ds(0, count)], dst_ref=h_got.at[zsel, pl.ds(0, count), src],
             send_sem=h_send.at[i, zsel], recv_sem=h_recv.at[i, zsel],
-            device_id=(s, zh * 8 + to), device_id_type=MESH,
-        )
-
-    def h_arrived(i, zsel):
-        src = (me8 + 8 - i) % 8
-        pltpu.make_async_remote_copy(
-            src_ref=h_v.at[0], dst_ref=h_got.at[zsel, :, src],
-            send_sem=h_send.at[i, zsel], recv_sem=h_recv.at[i, zsel],
-            device_id=sibling, device_id_type=MESH,
-        ).wait_recv()
-
-    for i in range(1, 8):
+            device_id=mate(i), device_id_type=MESH,
+        )
+
+    def hf_copy(i, src):
+        return pltpu.make_async_remote_copy(
+            src_ref=h_cross.at[(me8 + i) % 8], dst_ref=h_far.at[:, src],
+            send_sem=hf_send.at[i], recv_sem=hf_recv.at[i],
+            device_id=mate(i), device_id_type=MESH,
+        )
+
+    def begin_hidden():
+        for i in (2, 6, 4, 3, 7, 5, 1):
+            for zsel in (1, 0):
+                h_copy(i, zsel, me8).start()
         for zsel in range(2):
-            h_copy(i, zsel).start()
-    for zsel in range(2):
-        h_got[zsel, :, me8] = h_v[dp_of(zsel, 0, 0)]
-
-    lax.fori_loop(2, 6, plain(True, True), 0)
-    acc[...] = jnp.zeros_like(acc)
+            h_got[zsel, :, me8] = h_v[dp_of(zsel, 0, 0)]
+        acc[...] = jnp.zeros_like(acc)
+
+    def spread_hidden():
+        hidden_across.wait_recv()
+        for i in range(1, 8):
+            hf_copy(i, me8).start()
+        h_far[:, me8] = h_cross[me8]
 
     def gradient(t, carry):
-        for i in range(1, 8):
-            du_arrived(t, i)
+        for i in range(4):
+            du_copy(t, 2 * i + 1 - c, 0, sibling).wait_recv()
         du = du_all[t].reshape(HALF * ROW, R)
         for zsel in (1, 0):
             acc[zsel] += lax.dot_general(
@@ -309,14 +353,21 @@
             )
         return carry
 
-    for i in range(1, 8):
-        for zsel in range(2):
-            h_arrived(i, zsel)
-    lax.fori_loop(0, 4, gradient, 0)
-    stage(6, True, False)
-    lax.fori_loop(4, 6, gradient, 0)
-    stage(7, True, False)
-    lax.fori_loop(6, 8, gradient, 0)
+    def late_gradient(k):
+        for i in range(1, 8):
+            du_copy(EARLY + k, (me8 + i) % 8, 0, sibling).wait_recv()
+        acc[0] += lax.dot_general(
+            h_got[0, EARLY + k].reshape(HALF * ROW, BLK),
+            du_all[EARLY + k].reshape(HALF * ROW, R), TN, preferred_element_type=F32,
+        )
+
+    def far_gradient(k):
+        for i in range(1, 8):
+            far_copy(k, i, (me8 + i) % 8).wait_recv()
+        acc[0] += lax.dot_general(
+            h_far[k].reshape(HALF * ROW, BLK),
+            du_far[k].reshape(HALF * ROW, R), TN, preferred_element_type=F32,
+        )
 
     def z_copy(i):
         part = pl.ds(i * (BLK // 2), BLK // 2)
@@ -326,31 +377,56 @@
             device_id=across, device_id_type=MESH,
         )
 
-    for i in range(2):
-        part = pl.ds(i * (BLK // 2), BLK // 2)
-        z_out[part] = (acc[1, part] * SCALE).astype(BF16)
-        z_copy(i).start()
-    loads["first"].wait()
-    loads["second"].wait()
+    lax.fori_loop(0, 2, plain(False, True), 0)
+    begin_hidden()
+    lax.fori_loop(2, 5, plain(True, True), 0)
+    spread_hidden()
+    pass_rail(0)
+    pass_rail(1)
+    lax.fori_loop(5, 6, plain(True, True), 0)
+    pass_rail(2)
+    pass_rail(3)
+    for i in range(1, 8):
+        for zsel in range(2):
+            h_copy(i, zsel, (me8 + 8 - i) % 8).wait_recv()
+    lax.fori_loop(0, 3, gradient, 0)
+    pass_rail(4)
+
+    def finish_early():
+        pass_rail(5)
+        lax.fori_loop(3, EARLY, gradient, 0)
+        for i in range(2):
+            part = pl.ds(i * (BLK // 2), BLK // 2)
+            z_out[part] = (acc[1, part] * SCALE).astype(BF16)
+            z_copy(i).start()
+
+    for k in range(LATE):
+        stage(EARLY + k, True, False)
+        cross_copy(k).start()
+        for copy in spread(EARLY + k):
+            copy.start()
+        if k == 0:
+            finish_early()
+            spread_far(k)
+            for i in range(1, 8):
+                hf_copy(i, (me8 + 8 - i) % 8).wait_recv()
+            late_gradient(k)
+            far_gradient(k)
+    spread_far(LATE - 1)
+    late_gradient(LATE - 1)
+    far_gradient(LATE - 1)
+
     for i in range(2):
         part = pl.ds(i * (BLK // 2), BLK // 2)
         z_copy(i).wait_recv()
-        grad = acc[0, part] * SCALE + z_in[part].astype(F32)
-        moment_a = 0.9 * first_v[part].astype(F32) + 0.1 * grad
-        moment_b = 0.95 * second_v[part].astype(F32) + 0.05 * grad * grad
-        master = m_v[part]
-        master_out[part] = master - 0.02 * (
-            moment_a / (jnp.sqrt(moment_b) + 1e-08) + 0.1 * master
-        )
-        first_out[part] = moment_a.astype(BF16)
-        second_out[part] = moment_b.astype(BF16)
+        grad_out[part] = acc[0, part] * SCALE + z_in[part].astype(F32)
 
     for copy in sends:
         copy.wait_send()
 
     def sent(t, carry):
-        for i in range(1, 8):
-            du_copy(t, i).wait_send()
+        for copy in rail(t) + passed(t):
+            copy.wait_send()
         return carry
 
     def relayed(t, carry):
@@ -358,33 +434,35 @@
             relay_copy(t, n).wait_send()
         return carry
 
-    lax.fori_loop(0, STAGES, sent, 0)
-    lax.fori_loop(0, 6, relayed, 0)
+    lax.fori_loop(0, EARLY, sent, 0)
+    lax.fori_loop(0, EARLY, relayed, 0)
+    hidden_across.wait_send()
     for i in range(1, 8):
+        hf_copy(i, me8).wait_send()
         for zsel in range(2):
-            h_copy(i, zsel).wait_send()
+            h_copy(i, zsel, me8).wait_send()
+    for k in range(LATE):
+        cross_copy(k).wait_send()
+        for copy in spread(EARLY + k):
+            copy.wait_send()
+        for i in range(1, 8):
+            far_copy(k, i, me8).wait_send()
     for i in range(2):
         z_copy(i).wait_send()
 
 
 def on_device(section_inputs, grad_first, value_master, first_moment, second_moment, output_weight):
     dma = pltpu.SemaphoreType.DMA
-    outs = pl.pallas_call(
+    grad = pl.pallas_call(
         lap_kernel,
         name="lap",
-        out_shape=(
-            jax.ShapeDtypeStruct((BLK, R), F32),
-            jax.ShapeDtypeStruct((BLK, R), BF16),
-            jax.ShapeDtypeStruct((BLK, R), BF16),
-        ),
-        in_specs=[pl.BlockSpec(memory_space=pl.ANY)] * 6,
-        out_specs=[pl.BlockSpec(memory_space=pltpu.VMEM)] * 3,
+        out_shape=jax.ShapeDtypeStruct((BLK, R), F32),
+        in_specs=[pl.BlockSpec(memory_space=pl.ANY)] * 4,
+        out_specs=pl.BlockSpec(memory_space=pltpu.VMEM),
         scratch_shapes=[
             pltpu.VMEM((TOK, D), BF16),
             pltpu.VMEM((STAGES, CHUNKS, ROW, WIDE), BF16),
             pltpu.VMEM((BLK, R), F32),
-            pltpu.VMEM((BLK, R), BF16),
-            pltpu.VMEM((BLK, R), BF16),
             pltpu.VMEM((N_DP, BLK, R), BF16),
             pltpu.VMEM((N_DP, R, BLK), BF16),
             pltpu.VMEM((N_DP, STAGES, ROW, BLK), BF16),
@@ -393,12 +471,15 @@
             pltpu.VMEM((STAGES, ROW, R), F32),
             pltpu.VMEM((2, ROW, R), F32),
             pltpu.VMEM((STAGES, HALF, ROW, R), BF16),
+            pltpu.VMEM((LATE, HALF, ROW, R), BF16),
             pltpu.VMEM((2, STAGES, HALF, ROW, BLK), BF16),
+            pltpu.VMEM((HALF, LATE, ROW, BLK), BF16),
+            pltpu.VMEM((LATE, HALF, ROW, BLK), BF16),
             pltpu.VMEM((2, BLK, R), F32),
             pltpu.VMEM((BLK, R), BF16),
             pltpu.VMEM((BLK, R), BF16),
             pltpu.VMEM((6, CHUNKS, ROW, WIDE), BF16),
-            dma((5 + 2 * CHUNKS,)),
+            dma((3 + 2 * CHUNKS,)),
             dma((64,)),
             dma((4, N_DP)),
             dma((6, CHUNKS)),
@@ -407,15 +488,27 @@
             dma((8, 2)),
             dma((STAGES, 8)),
             dma((STAGES, 8)),
+            dma((LATE,)),
+            dma((LATE,)),
+            dma((LATE, 8)),
+            dma((LATE, 8)),
+            dma((8,)),
+            dma((8,)),
             dma((2,)),
             dma((2,)),
         ],
         compiler_params=pltpu.CompilerParams(
-            collective_id=0, has_side_effects=True, vmem_limit_bytes=48 * 1024 * 1024
+            collective_id=0, has_side_effects=True, vmem_limit_bytes=60 * 1024 * 1024
         ),
         cost_estimate=pl.CostEstimate(flops=4 * 10**9, bytes_accessed=5 * 2**20, transcendentals=0),
-    )(section_inputs, grad_first, value_master, first_moment, second_moment, output_weight)
-    return tuple(out[None] for out in outs)
+    )(section_inputs, grad_first, value_master, output_weight)
+    grad = grad[None]
+    moment_a = 0.9 * first_moment.astype(F32) + 0.1 * grad
+    moment_b = 0.95 * second_moment.astype(F32) + 0.05 * grad * grad
+    master = value_master - 0.02 * (
+        moment_a / (jnp.sqrt(moment_b) + 1e-08) + 0.1 * value_master
+    )
+    return master, moment_a.astype(BF16), moment_b.astype(BF16)
 
 
 def solution(mesh):

time: 139 us -> 126 us (0.906)
  local copies, waits for them, and re-layouts: 8.71 us -> 0.01 us
  Pallas kernels: 129 us -> 122 us
  other arithmetic: 0 us -> 2.45 us
    unnamed x15 -> x6, local copies, waits for them, and re-layouts: 8.71 us -> 0.01 us
    pallas_call x1, Pallas kernels: 129 us -> 122 us  [on_device(): pl.pallas_call(lap_kernel, name='lap', out_shape=jax.ShapeDtypeStruct((BL...]
    convert_element_type x0 -> x1, other arithmetic: none -> 2.45 us  [on_device(): return (master, moment_a.astype(BF16), moment_b.astype(BF16))]
where the time goes in v2:
time: 126 us; the launch traced here: 125 us
  Pallas kernels  122 us (97%)
  other arithmetic  2.45 us (2%)
    pallas_call x1, Pallas kernels, on_device(): pl.pallas_call(lap_kernel, name='lap', out_shape=jax.ShapeDtypeStruct((BL...  122 us

profile of v2, /device:TPU:1, one launch (start us, length us, event | category | flops | bytes accessed | tf_op | source)
XLA Modules:
  0.0 124.7 jit_solution(2713600265416001188)
XLA Ops:
  0.6 0.0 copy-start
  0.6 0.0 copy-start.1
  0.7 0.0 copy-start.2
  0.7 121.6 %lap.1 = f32[256,512]{1,0:T(8,128)} custom-call(bf16[1,256,4096]{2,1,0:T(8,128)(2,1)} %x_hbm.1, bf16[1,64,4096]{2,1,0:T(8,128)(2,1)} %g_hbm.1, f32[1,256,512]{2,1,0:T(8,128)} %m_hbm.1, bf16[1,512,256]{2,1,0:T(8,128)(2,1)} %ow_hbm.1), custom_call_target="tpu_custom_call" | custom-call | flops 4000000000 | bytes 5242880 | tf_op jit(solution)/shard_map/lap/pallas_call | solution.py:456
  122.2 0.0 copy-done
  122.3 0.0 copy-done.1
  122.3 0.0 copy-done.2
  122.3 2.5 %fusion.3 = (bf16[1,256,512]{2,1,0:T(8,128)(2,1)}, f32[1,256,512]{2,1,0:T(8,128)}, bf16[1,256,512]{2,1,0:T(8,128)(2,1)}) fusion(f32[256,512]{1,0:T(8,128)} %lap.1, bf16[1,256,512]{2,1,0:T(8,128)(2,1)S(1)} %copy-done.1, f32[1,256,512]{2,1,0:T(8,128)S(1)} %copy-done, bf16[1,256,512]{2,1,0:T(8,128)(2,1)S(1)} %copy-done.2), kind=kLoop, calls=%fused_computation.6 | loop fusion | flops 2228224 | bytes 2621440 | tf_op jit(solution)/shard_map/convert_element_type | solution.py:511
Async XLA Ops:
  0.6 121.6 %copy-start = (f32[1,256,512]{2,1,0:T(8,128)S(1)}, f32[1,256,512]{2,1,0:T(8,128)}, u32[]{:S(2)}) copy-start(f32[1,256,512]{2,1,0:T(8,128)} %m_hbm.1) | copy-start | bytes 1572868
  0.6 121.6 %copy-start.1 = (bf16[1,256,512]{2,1,0:T(8,128)(2,1)S(1)}, bf16[1,256,512]{2,1,0:T(8,128)(2,1)}, u32[]{:S(2)}) copy-start(bf16[1,256,512]{2,1,0:T(8,128)(2,1)} %param.10) | copy-start | bytes 786436
  0.7 121.6 %copy-start.2 = (bf16[1,256,512]{2,1,0:T(8,128)(2,1)S(1)}, bf16[1,256,512]{2,1,0:T(8,128)(2,1)}, u32[]{:S(2)}) copy-start(bf16[1,256,512]{2,1,0:T(8,128)(2,1)} %param.9) | copy-start | bytes 786436

commit v3 on v2

--- a/solution.py
+++ b/solution.py
@@ -25,6 +25,8 @@
 HALF = 8
 EARLY = 6
 LATE = STAGES - EARLY
+BEFORE = 1
+PARTS = 4
 SCALE = 1.0 / math.sqrt(D)
 
 NT = (((1,), (1,)), ((), ()))
@@ -109,7 +111,7 @@
         ).wait_recv()
 
     for p in range(4):
-        for target in (across, right, left, sibling):
+        for target in ((across,) if p < 2 else ()) + (right, left, sibling):
             pass_on(p, d, target)
 
     def handle(p, zsel, dx):
@@ -144,7 +146,7 @@
         for n in range(CHUNKS):
             loads["g", t, n].wait()
 
-    def upper(zsel):
+    def upper(zsel, first=0, count=HALF):
         base = (zh if zsel == 0 else 1 - zh) * HALF
 
         def one(i, carry):
@@ -155,7 +157,7 @@
             u_v[...] += part.reshape(STAGES, ROW, R)
             return carry
 
-        lax.fori_loop(0, HALF, one, 0)
+        lax.fori_loop(first, first + count, one, 0)
 
     def onto(total, grads, n):
         for i in range(PER):
@@ -188,6 +190,10 @@
         (2, 0, -1), (2, 0, 1), (3, 0, -1), (3, 0, 1), (0, 0, 2), (1, 1, 0), (1, 0, 2),
     ):
         handle(*event)
+        if event == (2, 0, -1):
+            pass_on(2, d, across)
+        if event == (1, 1, 0):
+            pass_on(3, d, across)
     from_sibling((0, 1), 0)
     upper(0)
     for event in (
@@ -201,9 +207,6 @@
     hidden_across.start()
     for event in ((2, 1, -1), (2, 1, 1)):
         handle(*event)
-    from_sibling((0, 1), 1)
-    upper(1)
-
     def gate(t, carry):
         u = u_v[t] * SCALE
         sig = jax.nn.sigmoid(u)
@@ -211,9 +214,11 @@
         f_v[t] = sig * (1.0 + u * (1.0 - sig))
         return carry
 
+    from_sibling((0, 1), 1)
+    for i, event in enumerate(((3, 1, -1), (3, 1, 1), (2, 1, 2), (3, 1, 2))):
+        handle(*event)
+        upper(1, 2 * i, 2)
     lax.fori_loop(0, STAGES, gate, 0)
-    for event in ((2, 1, 2), (3, 1, -1), (3, 1, 1), (3, 1, 2)):
-        handle(*event)
     from_sibling((2, 3), 1)
     first_back(1)
 
@@ -241,9 +246,6 @@
             du_copy(t, me8, 0, sibling)
         ]
 
-    def spread(t):
-        return [du_copy(t, me8, i, mate(i)) for i in range(1, 8)]
-
     def passed(t):
         return [du_copy(t, (me8 + 2 * i) % 8, 3 + i, sibling) for i in (1, 3, 2)]
 
@@ -259,17 +261,30 @@
             device_id=across, device_id_type=MESH,
         )
 
-    def far_copy(k, i, src):
+    def far_copy(k, src, i, target):
         return pltpu.make_async_remote_copy(
             src_ref=du_far.at[k, src], dst_ref=du_far.at[k, src],
             send_sem=far_send.at[k, i], recv_sem=far_recv.at[k, src],
-            device_id=mate(i), device_id_type=MESH,
-        )
-
-    def spread_far(k):
+            device_id=target, device_id_type=MESH,
+        )
+
+    def far_rail(k):
+        return [far_copy(k, me8, i, mate(2 * i)) for i in (1, 3, 2)] + [
+            far_copy(k, me8, 0, sibling)
+        ]
+
+    def far_passed(k):
+        return [far_copy(k, (me8 + 2 * i) % 8, 3 + i, sibling) for i in (1, 3, 2)]
+
+    def begin_far(k):
         cross_copy(k).wait_recv()
-        for i in range(1, 8):
-            far_copy(k, i, me8).start()
+        for copy in far_rail(k):
+            copy.start()
+
+    def pass_far(k):
+        for copy in far_passed(k):
+            copy.wait_recv()
+            copy.start()
 
     def stage(t, arrives, leaves):
         if arrives:
@@ -354,100 +369,100 @@
         return carry
 
     def late_gradient(k):
-        for i in range(1, 8):
-            du_copy(EARLY + k, (me8 + i) % 8, 0, sibling).wait_recv()
+        for i in range(4):
+            du_copy(EARLY + k, 2 * i + 1 - c, 0, sibling).wait_recv()
         acc[0] += lax.dot_general(
             h_got[0, EARLY + k].reshape(HALF * ROW, BLK),
             du_all[EARLY + k].reshape(HALF * ROW, R), TN, preferred_element_type=F32,
         )
 
     def far_gradient(k):
-        for i in range(1, 8):
-            far_copy(k, i, (me8 + i) % 8).wait_recv()
+        for i in range(4):
+            far_copy(k, 2 * i + 1 - c, 0, sibling).wait_recv()
         acc[0] += lax.dot_general(
             h_far[k].reshape(HALF * ROW, BLK),
             du_far[k].reshape(HALF * ROW, R), TN, preferred_element_type=F32,
         )
 
     def z_copy(i):
-        part = pl.ds(i * (BLK // 2), BLK // 2)
+        part = pl.ds(i * (BLK // PARTS), BLK // PARTS)
         return pltpu.make_async_remote_copy(
             src_ref=z_out.at[part], dst_ref=z_in.at[part],
             send_sem=z_send.at[i], recv_sem=z_recv.at[i],
             device_id=across, device_id_type=MESH,
         )
 
-    lax.fori_loop(0, 2, plain(False, True), 0)
-    begin_hidden()
-    lax.fori_loop(2, 5, plain(True, True), 0)
-    spread_hidden()
-    pass_rail(0)
-    pass_rail(1)
-    lax.fori_loop(5, 6, plain(True, True), 0)
-    pass_rail(2)
-    pass_rail(3)
-    for i in range(1, 8):
-        for zsel in range(2):
-            h_copy(i, zsel, (me8 + 8 - i) % 8).wait_recv()
-    lax.fori_loop(0, 3, gradient, 0)
-    pass_rail(4)
-
-    def finish_early():
-        pass_rail(5)
-        lax.fori_loop(3, EARLY, gradient, 0)
-        for i in range(2):
-            part = pl.ds(i * (BLK // 2), BLK // 2)
-            z_out[part] = (acc[1, part] * SCALE).astype(BF16)
-            z_copy(i).start()
-
-    for k in range(LATE):
-        stage(EARLY + k, True, False)
+    def exchange(i):
+        part = pl.ds(i * (BLK // PARTS), BLK // PARTS)
+        z_out[part] = (acc[1, part] * SCALE).astype(BF16)
+        z_copy(i).start()
+
+    def late_stage(k):
+        t = EARLY + k
+        stage(t, True, t < STAGES - 2)
         cross_copy(k).start()
-        for copy in spread(EARLY + k):
+        for copy in rail(t):
             copy.start()
-        if k == 0:
-            finish_early()
-            spread_far(k)
-            for i in range(1, 8):
-                hf_copy(i, (me8 + 8 - i) % 8).wait_recv()
-            late_gradient(k)
-            far_gradient(k)
-    spread_far(LATE - 1)
-    late_gradient(LATE - 1)
-    far_gradient(LATE - 1)
-
-    for i in range(2):
-        part = pl.ds(i * (BLK // 2), BLK // 2)
-        z_copy(i).wait_recv()
-        grad_out[part] = acc[0, part] * SCALE + z_in[part].astype(F32)
-
-    for copy in sends:
-        copy.wait_send()
+
+    def relayed(t, carry):
+        for n in range(CHUNKS):
+            relay_copy(t, n).wait_send()
+        return carry
 
     def sent(t, carry):
         for copy in rail(t) + passed(t):
             copy.wait_send()
         return carry
 
-    def relayed(t, carry):
-        for n in range(CHUNKS):
-            relay_copy(t, n).wait_send()
-        return carry
-
+    lax.fori_loop(0, 2, plain(False, True), 0)
+    begin_hidden()
+    lax.fori_loop(2, EARLY, plain(True, True), 0)
+    late_stage(0)
+    for t in range(EARLY):
+        pass_rail(t)
+    for i in range(1, 8):
+        for zsel in range(2):
+            h_copy(i, zsel, (me8 + 8 - i) % 8).wait_recv()
+    lax.fori_loop(0, EARLY, gradient, 0)
+    for i in range(BEFORE):
+        exchange(i)
+    spread_hidden()
+    begin_far(0)
+    late_stage(1)
+    for i in range(BEFORE, PARTS):
+        exchange(i)
+    pass_rail(EARLY)
+    pass_far(0)
+    pass_rail(EARLY + 1)
+    begin_far(1)
+    for i in range(1, 8):
+        hf_copy(i, (me8 + 8 - i) % 8).wait_recv()
+    late_gradient(0)
+    far_gradient(0)
+    late_gradient(1)
+    for copy in sends:
+        copy.wait_send()
+    lax.fori_loop(0, STAGES - 2, relayed, 0)
     lax.fori_loop(0, EARLY, sent, 0)
-    lax.fori_loop(0, EARLY, relayed, 0)
-    hidden_across.wait_send()
     for i in range(1, 8):
         hf_copy(i, me8).wait_send()
         for zsel in range(2):
             h_copy(i, zsel, me8).wait_send()
+    hidden_across.wait_send()
+    pass_far(1)
+    far_gradient(1)
+
+    for i in range(PARTS):
+        part = pl.ds(i * (BLK // PARTS), BLK // PARTS)
+        z_copy(i).wait_recv()
+        grad_out[part] = acc[0, part] * SCALE + z_in[part].astype(F32)
+
+    lax.fori_loop(EARLY, STAGES, sent, 0)
     for k in range(LATE):
         cross_copy(k).wait_send()
-        for copy in spread(EARLY + k):
+        for copy in far_rail(k) + far_passed(k):
             copy.wait_send()
-        for i in range(1, 8):
-            far_copy(k, i, me8).wait_send()
-    for i in range(2):
+    for i in range(PARTS):
         z_copy(i).wait_send()
 
 
@@ -494,8 +509,8 @@
             dma((LATE, 8)),
             dma((8,)),
             dma((8,)),
-            dma((2,)),
-            dma((2,)),
+            dma((PARTS,)),
+            dma((PARTS,)),
         ],
         compiler_params=pltpu.CompilerParams(
             collective_id=0, has_side_effects=True, vmem_limit_bytes=60 * 1024 * 1024

time: 126 us -> 118 us (0.937)
  Pallas kernels: 122 us -> 114 us
    pallas_call x1, Pallas kernels: 122 us -> 114 us  [on_device(): pl.pallas_call(lap_kernel, name='lap', out_shape=jax.ShapeDtypeStruct((BL...]
where the time goes in v3:
time: 118 us; the launch traced here: 117 us
  Pallas kernels  114 us (97%)
  other arithmetic  2.45 us (2%)
    pallas_call x1, Pallas kernels, on_device(): pl.pallas_call(lap_kernel, name='lap', out_shape=jax.ShapeDtypeStruct((BL...  114 us
    convert_element_type x1, other arithmetic, on_device(): return (master, moment_a.astype(BF16), moment_b.astype(BF16))  2.45 us

profile of v3, /device:TPU:1, one launch (start us, length us, event | category | flops | bytes accessed | tf_op | source)
XLA Modules:
  0.0 117.3 jit_solution(11920440541204236447)
XLA Ops:
  0.6 0.0 copy-start
  0.6 0.0 copy-start.1
  0.7 0.0 copy-start.2
  0.7 114.1 %lap.1 = f32[256,512]{1,0:T(8,128)} custom-call(bf16[1,256,4096]{2,1,0:T(8,128)(2,1)} %x_hbm.1, bf16[1,64,4096]{2,1,0:T(8,128)(2,1)} %g_hbm.1, f32[1,256,512]{2,1,0:T(8,128)} %m_hbm.1, bf16[1,512,256]{2,1,0:T(8,128)(2,1)} %ow_hbm.1), custom_call_target="tpu_custom_call" | custom-call | flops 4000000000 | bytes 5242880 | tf_op jit(solution)/shard_map/lap/pallas_call | solution.py:471
  114.8 0.0 copy-done
  114.8 0.0 copy-done.1
  114.8 0.0 copy-done.2
  114.8 2.5 %fusion.3 = (bf16[1,256,512]{2,1,0:T(8,128)(2,1)}, f32[1,256,512]{2,1,0:T(8,128)}, bf16[1,256,512]{2,1,0:T(8,128)(2,1)}) fusion(f32[256,512]{1,0:T(8,128)} %lap.1, bf16[1,256,512]{2,1,0:T(8,128)(2,1)S(1)} %copy-done.1, f32[1,256,512]{2,1,0:T(8,128)S(1)} %copy-done, bf16[1,256,512]{2,1,0:T(8,128)(2,1)S(1)} %copy-done.2), kind=kLoop, calls=%fused_computation.6 | loop fusion | flops 2228224 | bytes 2621440 | tf_op jit(solution)/shard_map/convert_element_type | solution.py:526
Async XLA Ops:
  0.6 114.2 %copy-start = (f32[1,256,512]{2,1,0:T(8,128)S(1)}, f32[1,256,512]{2,1,0:T(8,128)}, u32[]{:S(2)}) copy-start(f32[1,256,512]{2,1,0:T(8,128)} %m_hbm.1) | copy-start | bytes 1572868
  0.6 114.2 %copy-start.1 = (bf16[1,256,512]{2,1,0:T(8,128)(2,1)S(1)}, bf16[1,256,512]{2,1,0:T(8,128)(2,1)}, u32[]{:S(2)}) copy-start(bf16[1,256,512]{2,1,0:T(8,128)(2,1)} %param.10) | copy-start | bytes 786436
  0.7 114.2 %copy-start.2 = (bf16[1,256,512]{2,1,0:T(8,128)(2,1)S(1)}, bf16[1,256,512]{2,1,0:T(8,128)(2,1)}, u32[]{:S(2)}) copy-start(bf16[1,256,512]{2,1,0:T(8,128)(2,1)} %param.9) | copy-start | bytes 786436

commit v4 on v3

--- a/solution.py
+++ b/solution.py
@@ -89,10 +89,12 @@
 
     sends = []
 
+    spans = ((0, 0, 128), (0, 128, 128), (1, 0, 256), (1, 256, 128), (1, 384, 128))
+    rightward = (True, False, True, False, False)
+
     def piece(p, owner):
-        if p < 2:
-            return w_all.at[owner, pl.ds(p * (BLK // 2), BLK // 2)]
-        return o_all.at[owner, pl.ds((p - 2) * (R // 2), R // 2)]
+        weight, start, size = spans[p]
+        return (o_all if weight else w_all).at[owner, pl.ds(start, size)]
 
     def pass_on(p, owner, target):
         copy = pltpu.make_async_remote_copy(
@@ -110,16 +112,16 @@
             device_id=sibling, device_id_type=MESH,
         ).wait_recv()
 
-    for p in range(4):
+    for p in range(5):
         for target in ((across,) if p < 2 else ()) + (right, left, sibling):
             pass_on(p, d, target)
 
     def handle(p, zsel, dx):
         owner = dp_of(zsel, dx, 0)
         arrived(p, owner)
-        if dx == 0 or (dx == -1 and p % 2 == 0):
+        if dx == 0 or (dx == -1 and rightward[p]):
             pass_on(p, owner, right)
-        if dx == 0 or (dx == 1 and p % 2 == 1):
+        if dx == 0 or (dx == 1 and not rightward[p]):
             pass_on(p, owner, left)
         pass_on(p, owner, sibling)
 
@@ -187,26 +189,27 @@
 
     for event in (
         (0, 0, -1), (0, 0, 1), (1, 0, -1), (1, 0, 1), (0, 1, 0),
-        (2, 0, -1), (2, 0, 1), (3, 0, -1), (3, 0, 1), (0, 0, 2), (1, 1, 0), (1, 0, 2),
+        (2, 0, -1), (2, 0, 1), (3, 0, -1), (3, 0, 1),
+        (4, 0, -1), (4, 0, 1), (0, 0, 2), (1, 1, 0), (1, 0, 2),
     ):
         handle(*event)
         if event == (2, 0, -1):
             pass_on(2, d, across)
         if event == (1, 1, 0):
             pass_on(3, d, across)
+            pass_on(4, d, across)
     from_sibling((0, 1), 0)
     upper(0)
     for event in (
-        (2, 0, 2), (3, 0, 2), (0, 1, -1), (0, 1, 1), (2, 1, 0),
+        (2, 0, 2), (3, 0, 2), (4, 0, 2), (0, 1, -1), (0, 1, 1), (2, 1, 0),
         (1, 1, -1), (1, 1, 1), (0, 1, 2), (1, 1, 2),
     ):
         handle(*event)
-    from_sibling((2, 3), 0)
+    from_sibling((2, 3, 4), 0)
     first_back(0)
-    handle(3, 1, 0)
+    for event in ((3, 1, 0), (2, 1, -1), (2, 1, 1), (4, 1, 0)):
+        handle(*event)
     hidden_across.start()
-    for event in ((2, 1, -1), (2, 1, 1)):
-        handle(*event)
     def gate(t, carry):
         u = u_v[t] * SCALE
         sig = jax.nn.sigmoid(u)
@@ -215,11 +218,16 @@
         return carry
 
     from_sibling((0, 1), 1)
-    for i, event in enumerate(((3, 1, -1), (3, 1, 1), (2, 1, 2), (3, 1, 2))):
+    for event in ((3, 1, -1), (3, 1, 1)):
         handle(*event)
-        upper(1, 2 * i, 2)
+    upper(1, 0, 4)
+    for event in ((4, 1, -1), (4, 1, 1)):
+        handle(*event)
+    upper(1, 4, 4)
+    for event in ((2, 1, 2), (3, 1, 2), (4, 1, 2)):
+        handle(*event)
     lax.fori_loop(0, STAGES, gate, 0)
-    from_sibling((2, 3), 1)
+    from_sibling((2, 3, 4), 1)
     first_back(1)
 
     def relay_copy(t, n):
@@ -427,14 +435,14 @@
     for i in range(BEFORE):
         exchange(i)
     spread_hidden()
-    begin_far(0)
     late_stage(1)
     for i in range(BEFORE, PARTS):
         exchange(i)
+    begin_far(0)
     pass_rail(EARLY)
-    pass_far(0)
     pass_rail(EARLY + 1)
     begin_far(1)
+    pass_far(0)
     for i in range(1, 8):
         hf_copy(i, (me8 + 8 - i) % 8).wait_recv()
     late_gradient(0)
@@ -495,8 +503,8 @@
             pltpu.VMEM((BLK, R), BF16),
             pltpu.VMEM((6, CHUNKS, ROW, WIDE), BF16),
             dma((3 + 2 * CHUNKS,)),
-            dma((64,)),
-            dma((4, N_DP)),
+            dma((80,)),
+            dma((5, N_DP)),
             dma((6, CHUNKS)),
             dma((6, CHUNKS)),
             dma((8, 2)),

time: 118 us -> 117 us (level)
  no operation moved by 1% of the time
where the time goes in v4:
time: 117 us; the launch traced here: 116 us
  Pallas kernels  113 us (97%)
  other arithmetic  2.45 us (2%)
    pallas_call x1, Pallas kernels, on_device(): pl.pallas_call(lap_kernel, name='lap', out_shape=jax.ShapeDtypeStruct((BL...  113 us
    convert_element_type x1, other arithmetic, on_device(): return (master, moment_a.astype(BF16), moment_b.astype(BF16))  2.45 us

profile of v4, /device:TPU:1, one launch (start us, length us, event | category | flops | bytes accessed | tf_op | source)
XLA Modules:
  0.0 116.5 jit_solution(12815839966908978086)
XLA Ops:
  0.6 0.0 copy-start
  0.6 0.0 copy-start.1
  0.7 0.0 copy-start.2
  0.7 113.3 %lap.1 = f32[256,512]{1,0:T(8,128)} custom-call(bf16[1,256,4096]{2,1,0:T(8,128)(2,1)} %x_hbm.1, bf16[1,64,4096]{2,1,0:T(8,128)(2,1)} %g_hbm.1, f32[1,256,512]{2,1,0:T(8,128)} %m_hbm.1, bf16[1,512,256]{2,1,0:T(8,128)(2,1)} %ow_hbm.1), custom_call_target="tpu_custom_call" | custom-call | flops 4000000000 | bytes 5242880 | tf_op jit(solution)/shard_map/lap/pallas_call | solution.py:479
  114.0 0.0 copy-done
  114.0 0.0 copy-done.1
  114.0 0.0 copy-done.2
  114.0 2.5 %fusion.3 = (bf16[1,256,512]{2,1,0:T(8,128)(2,1)}, f32[1,256,512]{2,1,0:T(8,128)}, bf16[1,256,512]{2,1,0:T(8,128)(2,1)}) fusion(f32[256,512]{1,0:T(8,128)} %lap.1, bf16[1,256,512]{2,1,0:T(8,128)(2,1)S(1)} %copy-done.1, f32[1,256,512]{2,1,0:T(8,128)S(1)} %copy-done, bf16[1,256,512]{2,1,0:T(8,128)(2,1)S(1)} %copy-done.2), kind=kLoop, calls=%fused_computation.6 | loop fusion | flops 2228224 | bytes 2621440 | tf_op jit(solution)/shard_map/convert_element_type | solution.py:534
Async XLA Ops:
  0.6 113.4 %copy-start = (f32[1,256,512]{2,1,0:T(8,128)S(1)}, f32[1,256,512]{2,1,0:T(8,128)}, u32[]{:S(2)}) copy-start(f32[1,256,512]{2,1,0:T(8,128)} %m_hbm.1) | copy-start | bytes 1572868
  0.6 113.4 %copy-start.1 = (bf16[1,256,512]{2,1,0:T(8,128)(2,1)S(1)}, bf16[1,256,512]{2,1,0:T(8,128)(2,1)}, u32[]{:S(2)}) copy-start(bf16[1,256,512]{2,1,0:T(8,128)(2,1)} %param.10) | copy-start | bytes 786436
  0.7 113.4 %copy-start.2 = (bf16[1,256,512]{2,1,0:T(8,128)(2,1)S(1)}, bf16[1,256,512]{2,1,0:T(8,128)(2,1)}, u32[]{:S(2)}) copy-start(bf16[1,256,512]{2,1,0:T(8,128)(2,1)} %param.9) | copy-start | bytes 786436

commit v5 on v4

--- a/solution.py
+++ b/solution.py
@@ -96,14 +96,16 @@
         weight, start, size = spans[p]
         return (o_all if weight else w_all).at[owner, pl.ds(start, size)]
 
-    def pass_on(p, owner, target):
+    def pass_on(p, owner, target, now=True):
         copy = pltpu.make_async_remote_copy(
             src_ref=piece(p, owner), dst_ref=piece(p, owner),
             send_sem=ag_send.at[len(sends)], recv_sem=ag_recv.at[p, owner],
             device_id=target, device_id_type=MESH,
         )
-        copy.start()
         sends.append(copy)
+        if now:
+            copy.start()
+        return copy
 
     def arrived(p, owner):
         pltpu.make_async_remote_copy(
@@ -193,8 +195,11 @@
         (4, 0, -1), (4, 0, 1), (0, 0, 2), (1, 1, 0), (1, 0, 2),
     ):
         handle(*event)
+        if event == (1, 0, 1):
+            held = pass_on(2, d, across, False)
+            pl.when(s % 8 != 0)(held.start)
         if event == (2, 0, -1):
-            pass_on(2, d, across)
+            pl.when(s % 8 == 0)(held.start)
         if event == (1, 1, 0):
             pass_on(3, d, across)
             pass_on(4, d, across)
@@ -277,11 +282,15 @@
         )
 
     def far_rail(k):
+        if k == LATE - 1:
+            return [far_copy(k, me8, i, mate(i)) for i in (2, 6, 4, 3, 7, 5, 1)]
         return [far_copy(k, me8, i, mate(2 * i)) for i in (1, 3, 2)] + [
             far_copy(k, me8, 0, sibling)
         ]
 
     def far_passed(k):
+        if k == LATE - 1:
+            return []
         return [far_copy(k, (me8 + 2 * i) % 8, 3 + i, sibling) for i in (1, 3, 2)]
 
     def begin_far(k):
@@ -385,8 +394,12 @@
         )
 
     def far_gradient(k):
-        for i in range(4):
-            far_copy(k, 2 * i + 1 - c, 0, sibling).wait_recv()
+        if k == LATE - 1:
+            sources = [(me8 + i) % 8 for i in range(1, 8)]
+        else:
+            sources = [2 * i + 1 - c for i in range(4)]
+        for src in sources:
+            far_copy(k, src, 0, sibling).wait_recv()
         acc[0] += lax.dot_general(
             h_far[k].reshape(HALF * ROW, BLK),
             du_far[k].reshape(HALF * ROW, R), TN, preferred_element_type=F32,
@@ -457,19 +470,18 @@
         for zsel in range(2):
             h_copy(i, zsel, me8).wait_send()
     hidden_across.wait_send()
-    pass_far(1)
     far_gradient(1)
-
-    for i in range(PARTS):
-        part = pl.ds(i * (BLK // PARTS), BLK // PARTS)
-        z_copy(i).wait_recv()
-        grad_out[part] = acc[0, part] * SCALE + z_in[part].astype(F32)
 
     lax.fori_loop(EARLY, STAGES, sent, 0)
     for k in range(LATE):
         cross_copy(k).wait_send()
         for copy in far_rail(k) + far_passed(k):
             copy.wait_send()
+    for i in range(PARTS):
+        part = pl.ds(i * (BLK // PARTS), BLK // PARTS)
+        z_copy(i).wait_recv()
+        grad_out[part] = acc[0, part] * SCALE + z_in[part].astype(F32)
+
     for i in range(PARTS):
         z_copy(i).wait_send()
 

time: 117 us -> 117 us (level)
  no operation moved by 1% of the time
where the time goes in v5:
time: 117 us
  Pallas kernels  114 us (97%)
  other arithmetic  2.45 us (2%)
    pallas_call x1, Pallas kernels, on_device(): pl.pallas_call(lap_kernel, name='lap', out_shape=jax.ShapeDtypeStruct((BL...  114 us
    convert_element_type x1, other arithmetic, on_device(): return (master, moment_a.astype(BF16), moment_b.astype(BF16))  2.45 us

profile of v5, /device:TPU:1, one launch (start us, length us, event | category | flops | bytes accessed | tf_op | source)
XLA Modules:
  0.0 116.8 jit_solution(15617661351692097971)
XLA Ops:
  0.6 0.0 copy-start
  0.6 0.0 copy-start.1
  0.7 0.0 copy-start.2
  0.7 113.6 %lap.1 = f32[256,512]{1,0:T(8,128)} custom-call(bf16[1,256,4096]{2,1,0:T(8,128)(2,1)} %x_hbm.1, bf16[1,64,4096]{2,1,0:T(8,128)(2,1)} %g_hbm.1, f32[1,256,512]{2,1,0:T(8,128)} %m_hbm.1, bf16[1,512,256]{2,1,0:T(8,128)(2,1)} %ow_hbm.1), custom_call_target="tpu_custom_call" | custom-call | flops 4000000000 | bytes 5242880 | tf_op jit(solution)/shard_map/lap/pallas_call | solution.py:491
  114.3 0.0 copy-done
  114.3 0.0 copy-done.1
  114.3 0.0 copy-done.2
  114.3 2.5 %fusion.3 = (bf16[1,256,512]{2,1,0:T(8,128)(2,1)}, f32[1,256,512]{2,1,0:T(8,128)}, bf16[1,256,512]{2,1,0:T(8,128)(2,1)}) fusion(f32[256,512]{1,0:T(8,128)} %lap.1, bf16[1,256,512]{2,1,0:T(8,128)(2,1)S(1)} %copy-done.1, f32[1,256,512]{2,1,0:T(8,128)S(1)} %copy-done, bf16[1,256,512]{2,1,0:T(8,128)(2,1)S(1)} %copy-done.2), kind=kLoop, calls=%fused_computation.6 | loop fusion | flops 2228224 | bytes 2621440 | tf_op jit(solution)/shard_map/convert_element_type | solution.py:546
Async XLA Ops:
  0.6 113.7 %copy-start = (f32[1,256,512]{2,1,0:T(8,128)S(1)}, f32[1,256,512]{2,1,0:T(8,128)}, u32[]{:S(2)}) copy-start(f32[1,256,512]{2,1,0:T(8,128)} %m_hbm.1) | copy-start | bytes 1572868
  0.6 113.7 %copy-start.1 = (bf16[1,256,512]{2,1,0:T(8,128)(2,1)S(1)}, bf16[1,256,512]{2,1,0:T(8,128)(2,1)}, u32[]{:S(2)}) copy-start(bf16[1,256,512]{2,1,0:T(8,128)(2,1)} %param.10) | copy-start | bytes 786436
  0.7 113.7 %copy-start.2 = (bf16[1,256,512]{2,1,0:T(8,128)(2,1)S(1)}, bf16[1,256,512]{2,1,0:T(8,128)(2,1)}, u32[]{:S(2)}) copy-start(bf16[1,256,512]{2,1,0:T(8,128)(2,1)} %param.9) | copy-start | bytes 786436
